TPU v7x, 256 devices: a whole 4x4x8 slice. The times are simulated.
256 devices in a mesh: pipe: 4 (over x), expert: 64 (over z, y, core).
Axes of the slice: x: 4, y: 4, z: 8, core: 2. Of those that a mesh axis runs over, the one named last changes fastest.
Arguments:
- fwd_input: bfloat16 [4, 1024, 3584], P('pipe', 'expert'), may hold values from -6 to 6
- fwd_routes: int32 [4, 1024, 8], P('pipe', 'expert'), may hold values from 0 to 31, all different within a row; in each aligned block of 16 rows (0 to 15, 16 to 31, ..., all dimensions but the last counted through in order) at most 6 rows name the same one
- fwd_weight: float32 [4, 1024, 8], P('pipe', 'expert'), may hold values from 0.1 to 1
- bwd_input: bfloat16 [4, 1024, 3584], P('pipe', 'expert'), may hold values from -6 to 6
- bwd_grad: bfloat16 [4, 1024, 3584], P('pipe', 'expert'), may hold values from -6 to 6
- bwd_routes: int32 [4, 1024, 8], P('pipe', 'expert'), may hold values from 0 to 31, all different within a row; in each aligned block of 16 rows (0 to 15, 16 to 31, ..., all dimensions but the last counted through in order) at most 6 rows name the same one
- bwd_weight: float32 [4, 1024, 8], P('pipe', 'expert'), may hold values from 0.1 to 1
- w_gate: bfloat16 [4, 64, 3584, 512], P('pipe', 'expert'), may hold values from -0.09375 to 0.09375
- w_up: bfloat16 [4, 64, 3584, 512], P('pipe', 'expert'), may hold values from -0.09375 to 0.09375
- w_down: bfloat16 [4, 64, 512, 3584], P('pipe', 'expert'), may hold values from -0.1875 to 0.1875
Outputs:
- fwd_next: bfloat16 [4, 1024, 3584], P('pipe', 'expert')
- grad_prev: bfloat16 [4, 1024, 3584], P('pipe', 'expert')
Inputs may be any that keep to these rules, and one draw needn't show every extreme that they name: `fwd_routes`: the 16 tokens of one device name one expert at most 6 times; in every draw some expert is named exactly 6 times by one device's tokens. A token's 8 experts differ. `bwd_routes`: as for fwd_routes.
All inputs are finite; a program needn't handle non-finite values.
Results may differ from a plain program's by a relative error of at most 0.0058.
Values may be sent and summed in bfloat16 or wider, within the bound.
A program may use at most 128 MiB of HBM per device.

v0:
```python
import jax
import jax.numpy as jnp
from jax import lax
from jax.sharding import PartitionSpec as P

SPLIT = 2
E = 32
CAP = 6


def from_behind(shard, axis, by):
    length = lax.axis_size(axis)
    pairs = [(i, i + by) for i in range(length) if 0 <= i + by < length]
    return lax.ppermute(shard, axis, pairs)


def routing_tables(routes, weights, experts, capacity):
    matched = routes[:, :, None] == jnp.arange(experts, dtype=jnp.int32)[None, None, :]
    hit_count = jnp.sum(matched.astype(jnp.int32), axis=1)
    shares = jnp.sum(jnp.where(matched, weights[:, :, None], 0.0), axis=1)
    before = jnp.cumsum(hit_count, axis=0) - hit_count
    placed = (hit_count[:, :, None] == 1) & (
        before[:, :, None] == jnp.arange(capacity, dtype=jnp.int32)[None, None, :]
    )
    return (placed, shares)


def pack_rows(placed, tokens):
    tok_count, experts, capacity = placed.shape
    feat_width = tokens.shape[1]
    onehot = placed.astype(jnp.bfloat16)
    packed = jnp.einsum("tec,td->ecd", onehot, tokens, preferred_element_type=jnp.float32).astype(
        jnp.bfloat16
    )
    spread_out = jnp.broadcast_to(packed[:, None], (experts, SPLIT, capacity, feat_width))
    return spread_out.reshape(experts * SPLIT, capacity, feat_width)


def gather_rows(received, units_dev):
    per_group = min(units_dev, SPLIT)
    groups = units_dev // per_group
    senders = lax.axis_size("expert")
    slot_count = received[0].shape[1]
    return tuple(
        (
            member.reshape(senders, groups, per_group, slot_count, member.shape[2])[:, :, 0]
            for member in received
        )
    )


def expert_forward(row_block, gate_w, up_w, down_w):
    gate_val = jnp.einsum("ngcd,gsdf->ngscf", row_block, gate_w, preferred_element_type=jnp.float32)
    up_val = jnp.einsum("ngcd,gsdf->ngscf", row_block, up_w, preferred_element_type=jnp.float32)
    hidden = (jax.nn.silu(gate_val) * up_val).astype(jnp.bfloat16)
    return jnp.einsum("ngscf,gsfd->ngcd", hidden, down_w, preferred_element_type=jnp.float32)


def expert_backward(row_block, grad_block, gate_w, up_w, down_w):
    gate_val = jnp.einsum("ngcd,gsdf->ngscf", row_block, gate_w, preferred_element_type=jnp.float32)
    up_val = jnp.einsum("ngcd,gsdf->ngscf", row_block, up_w, preferred_element_type=jnp.float32)
    sigma = jax.nn.sigmoid(gate_val)
    hid_grad = jnp.einsum(
        "ngcd,gsfd->ngscf", grad_block, down_w, preferred_element_type=jnp.float32
    )
    gate_grad = (hid_grad * up_val * sigma * (1.0 + gate_val * (1.0 - sigma))).astype(jnp.bfloat16)
    up_grad = (hid_grad * gate_val * sigma).astype(jnp.bfloat16)
    result = jnp.einsum("ngscf,gsdf->ngcd", gate_grad, gate_w, preferred_element_type=jnp.float32)
    return result + jnp.einsum(
        "ngscf,gsdf->ngcd", up_grad, up_w, preferred_element_type=jnp.float32
    )


def flat_groups(result):
    return result.reshape(result.shape[0] * result.shape[1], result.shape[2], result.shape[3])


def assemble_parts(returned):
    units, slot_count, width = returned.shape
    copies = units // E
    return returned.reshape(E, copies, slot_count, width).sum(axis=1).astype(jnp.bfloat16)


def combine_rows(parts, placed, shares):
    mixing = placed.astype(jnp.float32) * shares[:, :, None]
    combined = jnp.einsum(
        "tec,ecd->td", mixing, parts.astype(jnp.float32), precision=lax.Precision.HIGHEST
    )
    return combined.astype(jnp.bfloat16)


def local(
    fwd_input,
    fwd_routes,
    fwd_weight,
    bwd_input,
    bwd_grad,
    bwd_routes,
    bwd_weight,
    w_gate,
    w_up,
    w_down,
):
    units_dev = w_gate.shape[1]
    per_group = min(units_dev, SPLIT)
    groups = units_dev // per_group
    feat_width = w_gate.shape[2]
    hidden_width = w_gate.shape[3]
    gate_local = w_gate[0].reshape(groups, per_group, feat_width, hidden_width)
    up_local = w_up[0].reshape(groups, per_group, feat_width, hidden_width)
    down_local = w_down[0].reshape(groups, per_group, hidden_width, feat_width)
    placed_fwd, shares_fwd = routing_tables(fwd_routes[0], fwd_weight[0], E, CAP)
    send_fwd = pack_rows(placed_fwd, fwd_input[0])
    row_block = gather_rows(
        (lax.all_to_all(send_fwd, "expert", split_axis=0, concat_axis=0, tiled=True),), units_dev
    )[0]
    result = expert_forward(row_block, gate_local, up_local, down_local)
    back_fwd = lax.all_to_all(
        flat_groups(result), "expert", split_axis=0, concat_axis=0, tiled=True
    )
    section_out = combine_rows(assemble_parts(back_fwd), placed_fwd, shares_fwd)
    placed_bwd, shares_bwd = routing_tables(bwd_routes[0], bwd_weight[0], E, CAP)
    send_inputs = pack_rows(placed_bwd, bwd_input[0])
    send_grads = pack_rows(placed_bwd, bwd_grad[0])
    row_block, grad_block = gather_rows(
        (
            lax.all_to_all(send_inputs, "expert", split_axis=0, concat_axis=0, tiled=True),
            lax.all_to_all(send_grads, "expert", split_axis=0, concat_axis=0, tiled=True),
        ),
        units_dev,
    )
    result = expert_backward(row_block, grad_block, gate_local, up_local, down_local)
    back_bwd = lax.all_to_all(
        flat_groups(result), "expert", split_axis=0, concat_axis=0, tiled=True
    )
    section_grad = combine_rows(assemble_parts(back_bwd), placed_bwd, shares_bwd)
    fwd_next = from_behind(section_out[None], "pipe", 1)
    grad_prev = from_behind(section_grad[None], "pipe", -1)
    return (fwd_next, grad_prev)


def solution(mesh):
    in_specs = (
        P("pipe", "expert", None),
        P("pipe", "expert", None),
        P("pipe", "expert", None),
        P("pipe", "expert", None),
        P("pipe", "expert", None),
        P("pipe", "expert", None),
        P("pipe", "expert", None),
        P("pipe", "expert", None, None),
        P("pipe", "expert", None, None),
        P("pipe", "expert", None, None),
    )
    out_specs = (P("pipe", "expert", None), P("pipe", "expert", None))
    return jax.shard_map(local, mesh=mesh, in_specs=in_specs, out_specs=out_specs, check_vma=False)
```

profile of v0, /device:TPU:8, one launch (start us, length us, event | category | flops | bytes accessed | tf_op | source)
XLA Modules:
  0.0 638.0 jit_solution(6065189041855163308)
XLA Ops:
  0.6 0.8 copy.69
  2.2 0.8 copy.73
  2.9 2.1 broadcast_in_dim.64
  5.0 12.4 %all-to-all-start.3 = ((bf16[64,6,3584]{2,1,0:T(8,128)(2,1)}), bf16[64,6,3584]{2,1,0:T(8,128)(2,1)}, u32[]{:S(2)}, u32[]{:S(2)}) async-start(bf16[64,6,3584]{2,1,0:T(8,128)(2,1)} %bitcast.157), calls=%async_computation.3 | async-start | bytes 7340032 | tf_op jit(solution)/shard_map/all_to_all | solution.py:127
  18.0 0.8 copy.71
  18.8 83.6 %all-to-all-done.3 = bf16[64,6,3584]{2,1,0:T(8,128)(2,1)} async-done(((bf16[64,6,3584]{2,1,0:T(8,128)(2,1)}), bf16[64,6,3584]{2,1,0:T(8,128)(2,1)}, u32[]{:S(2)}, u32[]{:S(2)}) %all-to-all-start.3) | async-done | bytes 2752544 | tf_op jit(solution)/shard_map/all_to_all | solution.py:127
  102.3 2.1 broadcast_in_dim.63
  104.4 5.8 all-to-all-start.2
  111.0 0.8 copy.64
  111.8 83.4 %all-to-all-done.2 = bf16[64,6,3584]{2,1,0:T(8,128)(2,1)} async-done(((bf16[64,6,3584]{2,1,0:T(8,128)(2,1)}), bf16[64,6,3584]{2,1,0:T(8,128)(2,1)}, u32[]{:S(2)}, u32[]{:S(2)}) %all-to-all-start.2) | async-done | bytes 2752544 | tf_op jit(solution)/shard_map/all_to_all | solution.py:128
  195.2 2.1 broadcast_in_dim.59
  197.4 5.6 all-to-all-start
  203.0 4.9 fusion.44
  207.9 3.7 fusion.24
  211.6 9.8 %fusion.4 = f32[64,6,3584]{2,0,1:T(8,128)} fusion(bf16[1,1,3584,512]{3,2,1,0:T(8,128)(2,1)} %param.17, f32[64,1,1,6,512]{4,0,3,2,1:T(8,128)S(1)} %fusion.24, bf16[1,1,3584,512]{3,2,1,0:T(8,128)(2,1)} %param.18, bf16[64,6,3584]{2,1,0:T(8,128)(2,1)} %all-to-all-done.3, f32[64,1,1,6,512]{4,0,3,2,1:T(8,128)S(1)} %fusion.44), kind=kOutput, calls=%fused_computation.12 | convolution fusion | flops 2820538368 | bytes 17170432 | tf_op jit(solution)/shard_map/ngscf,gsdf->ngcd/dot_general | solution.py:68
  221.4 5.3 convolution_add_fusion
  226.7 6.3 copy.76
  233.0 55.0 %all-to-all-done = bf16[64,6,3584]{2,1,0:T(8,128)(2,1)} async-done(((bf16[64,6,3584]{2,1,0:T(8,128)(2,1)}), bf16[64,6,3584]{2,1,0:T(8,128)(2,1)}, u32[]{:S(2)}, u32[]{:S(2)}) %all-to-all-start) | async-done | bytes 2752544 | tf_op jit(solution)/shard_map/all_to_all | solution.py:115
  288.0 5.7 all-to-all-start.4
  293.8 4.7 fusion.39
  298.5 9.8 %fusion.17 = f32[64,6,3584]{2,0,1:T(8,128)} fusion(bf16[1,1,512,3584]{3,2,1,0:T(8,128)(2,1)} %param.19, bf16[1,1,3584,512]{3,2,1,0:T(8,128)(2,1)} %param.18, bf16[64,6,3584]{2,1,0:T(8,128)(2,1)} %all-to-all-done, f32[64,1,1,6,512]{4,0,3,2,1:T(8,128)S(1)} %fusion.39), kind=kOutput, calls=%fused_computation.25 | convolution fusion | flops 2819751936 | bytes 16384000 | tf_op jit(solution)/shard_map/ngscf,gsfd->ngcd/dot_general | solution.py:56
  308.3 8.8 %copy.67 = f32[64,6,3584]{2,1,0:T(8,128)} copy(f32[64,6,3584]{2,0,1:T(8,128)} %fusion.17) | data formatting | bytes 11010048 | tf_op jit(solution)/shard_map/ngscf,gsfd->ngcd/dot_general | solution.py:56
  317.1 139.2 %all-to-all-done.4 = f32[64,6,3584]{2,1,0:T(8,128)} async-done(((f32[64,6,3584]{2,1,0:T(8,128)}), f32[64,6,3584]{2,1,0:T(8,128)}, u32[]{:S(2)}, u32[]{:S(2)}) %all-to-all-start.4) | async-done | bytes 5505056 | tf_op jit(solution)/shard_map/all_to_all | solution.py:133
  456.3 7.3 %all-to-all-start.1 = ((f32[64,6,3584]{2,1,0:T(8,128)}), f32[64,6,3584]{2,1,0:T(8,128)}, u32[]{:S(2)}, u32[]{:S(2)}) async-start(f32[64,6,3584]{2,1,0:T(8,128)} %copy.67), calls=%async_computation.1 | async-start | bytes 14680064 | tf_op jit(solution)/shard_map/all_to_all | solution.py:118
  464.0 3.9 bitcast_reduce_fusion
  467.9 1.1 fusion.2
  469.0 1.3 collective-permute-start.1
  470.3 155.6 %all-to-all-done.1 = f32[64,6,3584]{2,1,0:T(8,128)} async-done(((f32[64,6,3584]{2,1,0:T(8,128)}), f32[64,6,3584]{2,1,0:T(8,128)}, u32[]{:S(2)}, u32[]{:S(2)}) %all-to-all-start.1) | async-done | bytes 5505056 | tf_op jit(solution)/shard_map/all_to_all | solution.py:118
  625.9 3.9 bitcast_reduce_fusion.1
  629.9 1.1 fusion.3
  631.0 3.4 collective-permute-start
  634.4 2.3 collective-permute-done
  (35 shorter events, 3.7 us)
Async XLA Ops:
  0.6 1.0 copy-start
  5.0 12.4 %copy-start.2 = (bf16[1,16,3584]{2,1,0:T(8,128)(2,1)S(1)}, bf16[1,16,3584]{2,1,0:T(8,128)(2,1)}, u32[]{:S(2)}) copy-start(bf16[1,16,3584]{2,1,0:T(8,128)(2,1)} %param.14) | copy-start | bytes 344068
  5.0 97.3 %all-to-all-start.3 = ((bf16[64,6,3584]{2,1,0:T(8,128)(2,1)}), bf16[64,6,3584]{2,1,0:T(8,128)(2,1)}, u32[]{:S(2)}, u32[]{:S(2)}) async-start(bf16[64,6,3584]{2,1,0:T(8,128)(2,1)} %bitcast.157), calls=%async_computation.3 | async-start | bytes 7340032 | tf_op jit(solution)/shard_map/all_to_all | solution.py:127
  104.4 5.8 copy-start.4
  104.4 6.0 copy-start.3
  104.4 90.8 %all-to-all-start.2 = ((bf16[64,6,3584]{2,1,0:T(8,128)(2,1)}), bf16[64,6,3584]{2,1,0:T(8,128)(2,1)}, u32[]{:S(2)}, u32[]{:S(2)}) async-start(bf16[64,6,3584]{2,1,0:T(8,128)(2,1)} %bitcast.155), calls=%async_computation.2 | async-start | bytes 7340032 | tf_op jit(solution)/shard_map/all_to_all | solution.py:128
  197.4 90.6 %all-to-all-start = ((bf16[64,6,3584]{2,1,0:T(8,128)(2,1)}), bf16[64,6,3584]{2,1,0:T(8,128)(2,1)}, u32[]{:S(2)}, u32[]{:S(2)}) async-start(bf16[64,6,3584]{2,1,0:T(8,128)(2,1)} %bitcast.156), calls=%async_computation | async-start | bytes 7340032 | tf_op jit(solution)/shard_map/all_to_all | solution.py:115
  203.0 4.9 copy-start.7
  288.0 168.3 %all-to-all-start.4 = ((f32[64,6,3584]{2,1,0:T(8,128)}), f32[64,6,3584]{2,1,0:T(8,128)}, u32[]{:S(2)}, u32[]{:S(2)}) async-start(f32[64,6,3584]{2,1,0:T(8,128)} %copy.76), calls=%async_computation.4 | async-start | bytes 14680064 | tf_op jit(solution)/shard_map/all_to_all | solution.py:133
  317.1 146.5 %copy-start.5 = (f32[1,16,8]{1,2,0:T(8,128)S(1)}, f32[1,16,8]{1,2,0:T(8,128)}, u32[]{:S(2)}) copy-start(f32[1,16,8]{1,2,0:T(8,128)} %param.16) | copy-start | bytes 1540
  317.1 146.6 %copy-start.6 = (f32[1,16,8]{1,2,0:T(8,128)S(1)}, f32[1,16,8]{1,2,0:T(8,128)}, u32[]{:S(2)}) copy-start(f32[1,16,8]{1,2,0:T(8,128)} %param.12) | copy-start | bytes 1540
  456.3 169.7 %all-to-all-start.1 = ((f32[64,6,3584]{2,1,0:T(8,128)}), f32[64,6,3584]{2,1,0:T(8,128)}, u32[]{:S(2)}, u32[]{:S(2)}) async-start(f32[64,6,3584]{2,1,0:T(8,128)} %copy.67), calls=%async_computation.1 | async-start | bytes 14680064 | tf_op jit(solution)/shard_map/all_to_all | solution.py:118
  467.9 170.1 %copy-start.1 = (bf16[1,16,3584]{2,1,0:T(8,128)(2,1)S(1)}, bf16[1,16,3584]{2,1,0:T(8,128)(2,1)}, u32[]{:S(2)}) copy-start(bf16[1,16,3584]{2,1,0:T(8,128)(2,1)} %param.13) | copy-start | bytes 344068
  469.0 165.4 %collective-permute-start.1 = (bf16[1,16,3584]{2,1,0:T(8,128)(2,1)S(1)}, bf16[1,16,3584]{2,1,0:T(8,128)(2,1)S(1)}, u32[]{:S(2)}, u32[]{:S(2)}) collective-permute-start(bf16[1,16,3584]{2,1,0:T(8,128)(2,1)S(1)} %fusion.2), channel_id=1, source_target_pairs={{64,0},{128,64},{192,128},{65,1},{129,65},{193,129},{66,2},{130,66... | collective-permute-start | bytes 344072 | tf_op jit(solution)/shard_map/ppermute | solution.py:14
  631.0 5.8 collective-permute-start
where the time goes:
time: 641 us; the launch traced here: 638 us
  waiting for transfers between devices  519 us (81%)
  matrix products  42 us (7%)
  starting transfers between devices  41.5 us (6%)
  local copies, waits for them, and re-layouts  26.1 us (4%)
  other arithmetic  8.37 us (1%)
    all_to_all x2, waiting for transfers between devices, local(): lax.all_to_all(flat_groups(result), 'expert', split_axis=0, concat_axis=0...  295 us
    all_to_all x1, waiting for transfers between devices, local(): lax.all_to_all(send_inputs, 'expert', split_axis=0, concat_axis=0, tiled=...  83.6 us
    all_to_all x1, waiting for transfers between devices, local(): lax.all_to_all(send_grads, 'expert', split_axis=0, concat_axis=0, tiled=T...  83.4 us
    all_to_all x1, waiting for transfers between devices, local(): lax.all_to_all(send_fwd, 'expert', split_axis=0, concat_axis=0, tiled=True)  55 us
    all_to_all x2, starting transfers between devices, local(): lax.all_to_all(flat_groups(result), 'expert', split_axis=0, concat_axis=0...  13.1 us
  transfers between devices with their start and end apart: 7, of which 6 were waited for; matrix products, arithmetic and copies ran while one was open for 10% of the time, Pallas kernels for 0%

commit v1 on v0

v1 whole, which is shorter than its diff:
```python
import functools

import jax
import jax.numpy as jnp
from jax import lax
from jax.experimental import pallas as pl
from jax.experimental.pallas import tpu as pltpu
from jax.sharding import PartitionSpec as P

MESH = pl.DeviceIdType.MESH
BF = jnp.bfloat16
F32 = jnp.float32

D = 3584
FF = 512
TOK = 16
CAP = 6
E = 32
TOP = 8
NX = 4
NZ = 8
NY = 4
SLOT = NZ * CAP
PLANE = NY * SLOT
ROWS = 2 * PLANE
GROUP = NZ * TOK
TILE = 256

HEAD = ((0, 512), (512, 1024), (1536, 1024), (2560, 1024))
TAIL = ((0, 1024), (1024, 1024), (2048, 1024), (3072, 512))
NH = len(HEAD)
NT = len(TAIL)
X, G, F = 0, 1, 2
B, O = 0, 1


def dot(a, b):
    return jnp.dot(a, b, preferred_element_type=F32)


def dot_nt(a, b):
    return lax.dot_general(a, b, (((1,), (1,)), ((), ())), preferred_element_type=F32)


def slots_and_shares(routes, weights):
    expert = lax.broadcasted_iota(jnp.int32, (TOK, 128), 1) & (E - 1)
    hit = jnp.zeros((TOK, 128), F32)
    share = jnp.zeros((TOK, 128), F32)
    for k in range(TOP):
        same = routes[:, k : k + 1] == expert
        hit = hit + jnp.where(same, 1.0, 0.0)
        share = share + jnp.where(same, weights[:, k : k + 1], 0.0)
    rows = lax.broadcasted_iota(jnp.int32, (TOK, TOK), 0)
    cols = lax.broadcasted_iota(jnp.int32, (TOK, TOK), 1)
    before = dot(jnp.where(rows > cols, 1.0, 0.0).astype(BF), hit.astype(BF))
    return jnp.where(hit > 0.5, before, -1.0), share


def kernel(
    xf, rf, wf, xb, gb, rb, wb, wg_h, wu_h, wd_h,
    out_f, out_b,
    wg, wu, wd, meta, onehot, mix_hi, mix_lo, ag, send, recv,
    gate, up, hid_a, hid_b, own, sib_s, sib_r, ret_s, ret_r, part, rs_s, rs_r, xs, xr,
    w_sem, m_ss, m_rs, z_ss, z_rs, y_ss, y_rs, d_ss, d_rs,
    p_ss, p_rs, r_ss, r_rs, c_ss, c_rs, x_ss, x_rs,
):
    px = lax.axis_index("pipe")
    e = lax.axis_index("expert")
    c = lax.rem(e, 2)
    y = lax.rem(lax.div(e, 2), NY)
    z = lax.div(e, 2 * NY)
    turn = 1 - 2 * c

    def at(qx, qz, qy, qc):
        return (lax.rem(qx + NX, NX), (lax.rem(qz + NZ, NZ) * NY + lax.rem(qy + NY, NY)) * 2 + qc)

    ahead = at(px, z + turn, y, c)
    behind = at(px, z - turn, y, c)
    ups = [None] + [at(px, z, y + i, c) for i in range(1, NY)]
    downs = [None] + [at(px, z, y - i, c) for i in range(1, NY)]
    sibling = at(px, z, y, 1 - c)
    x_next = at(px + 1, z, y, c)
    x_prev = at(px - 1, z, y, c)

    def remote(src, dst, ss, rs, device):
        return pltpu.make_async_remote_copy(
            src_ref=src, dst_ref=dst, send_sem=ss, recv_sem=rs, device_id=device, device_id_type=MESH
        )

    def take(ref, rs, device):
        remote(ref, ref, rs, rs, device).wait_recv()

    def sent(ref, ss, device):
        remote(ref, ref, ss, ss, device).wait_send()

    weight_copies = [
        pltpu.make_async_copy(a, b, w_sem.at[i])
        for i, (a, b) in enumerate(((wg_h, wg), (wu_h, wu), (wd_h, wd)))
    ]
    for copy in weight_copies:
        copy.start()

    barrier = pltpu.get_barrier_semaphore()
    partners = [ahead, behind, ups[1], ups[2], ups[3], sibling, x_next, x_prev]
    for device in partners:
        pl.semaphore_signal(barrier, inc=1, device_id=device, device_id_type=MESH)

    lane = lax.broadcasted_iota(jnp.int32, (TOK, 128), 1)
    pos_f, share_f = slots_and_shares(rf[...], wf[...])
    pos_b, share_b = slots_and_shares(rb[...], wb[...])
    meta[0:TOK, :] = jnp.where(
        lane < E, pos_f, jnp.where(lane < 2 * E, share_f, jnp.where(lane < 3 * E, pos_b, share_b))
    )
    pl.semaphore_wait(barrier, len(partners))

    def rows(block):
        return pl.ds(block * TOK, TOK)

    def meta_hop(src, dst, device):
        remote(meta.at[rows(src)], meta.at[rows(dst)], m_ss, m_rs.at[dst - 1], device).start()

    def hop(a, src, dst, k, device):
        cols = pl.ds(*HEAD[k])
        block = (xb, gb, xf)[a].at[:, cols] if src == 0 else ag.at[a, rows(src), cols]
        remote(block, ag.at[a, rows(dst), cols], z_ss.at[a], z_rs.at[a, dst - 1, k], device).start()

    def landed(a, block, k):
        take(ag.at[a, rows(block), pl.ds(*HEAD[k])], z_rs.at[a, block - 1, k], behind)

    def first_hops(a):
        for k in range(NH):
            hop(a, 0, 1, k, ahead)
            hop(a, 0, 7, k, behind)

    def forward_hops(a, with_meta=False):
        for s in (1, 2, 3):
            if with_meta:
                take(meta.at[rows(s)], m_rs.at[s - 1], behind)
                meta_hop(s, s + 1, ahead)
                take(meta.at[rows(8 - s)], m_rs.at[7 - s], ahead)
                if s < 3:
                    meta_hop(8 - s, 7 - s, behind)
            for k in range(NH):
                landed(a, s, k)
                hop(a, s, s + 1, k, ahead)
                landed(a, 8 - s, k)
                if s < 3:
                    hop(a, 8 - s, 7 - s, k, behind)

    def build(which):
        every = meta[...]
        lane = lax.broadcasted_iota(jnp.int32, (GROUP, 128), 1)
        base = 2 * E * (1 - which) + z * NY

        def column(off):
            return jnp.sum(jnp.where(lane == off, every, 0.0), axis=1, keepdims=True)

        r = lax.broadcasted_iota(jnp.int32, (GROUP, TILE), 1)
        t = lax.broadcasted_iota(jnp.int32, (GROUP, TILE), 0)
        j = jnp.zeros_like(r)
        for i in range(1, NY):
            j = j + jnp.where(r >= i * SLOT, 1, 0)
        r = r - j * SLOT
        source = jnp.zeros_like(r)
        for i in range(1, NZ):
            source = source + jnp.where(r >= i * CAP, 1, 0)
        slot = (r - source * CAP).astype(F32)
        pos = jnp.zeros((GROUP, TILE), F32)
        share = jnp.zeros((GROUP, TILE), F32)
        for i in range(NY):
            off = base + lax.rem(y + i, NY)
            pos = jnp.where(j == i, column(off), pos)
            share = jnp.where(j == i, column(off + E), share)
        match = jnp.logical_and(lax.shift_right_logical(t, 4) == source, pos == slot)
        onehot[which] = jnp.where(match, 1.0, 0.0).T[0:PLANE].astype(BF)
        share = jnp.where(match, share, 0.0)
        high = share.astype(BF)
        mix_hi[which] = high[:, 0:PLANE]
        mix_lo[which] = (share - high.astype(F32)).astype(BF)[:, 0:PLANE]

    def gather(a, k):
        which = 1 if a == F else 0
        cols = pl.ds(*HEAD[k])
        landed(a, 4, k)
        picked = dot(onehot[which], ag[a, :, cols]).astype(BF)
        recv[a, 0:SLOT, cols] = picked[0:SLOT]
        send[a, :, cols] = picked[SLOT:PLANE]

    def dispatch(a, k):
        cols = pl.ds(*HEAD[k])
        for i in range(1, NY):
            remote(
                send.at[a, pl.ds((i - 1) * SLOT, SLOT), cols],
                recv.at[a, pl.ds(i * SLOT, SLOT), cols],
                y_ss.at[a], y_rs.at[a, k], ups[i],
            ).start()

    def arrived(a, k):
        cols = pl.ds(*HEAD[k])
        take(recv.at[a, pl.ds(SLOT, PLANE - SLOT), cols], y_rs.at[a, k], ups[1])
        remote(
            recv.at[a, pl.ds(0, PLANE), cols], recv.at[a, pl.ds(PLANE, PLANE), cols],
            d_ss.at[a], d_rs.at[a, k], sibling,
        ).start()

    def complete(a):
        for k in range(NH):
            take(recv.at[a, pl.ds(PLANE, PLANE), pl.ds(*HEAD[k])], d_rs.at[a, k], sibling)

    for k in (0,):
        meta_hop(0, 1, ahead)
        meta_hop(0, 7, behind)
    first_hops(X)
    ag[X, 0:TOK, :] = xb[...]
    ag[G, 0:TOK, :] = gb[...]
    ag[F, 0:TOK, :] = xf[...]
    forward_hops(X, with_meta=True)
    first_hops(G)
    take(meta.at[rows(4)], m_rs.at[3], behind)
    build(0)
    for k in range(NH):
        gather(X, k)
        dispatch(X, k)
    forward_hops(G)
    first_hops(F)
    for k in range(NH):
        gather(G, k)
        dispatch(G, k)
    build(1)
    forward_hops(F)
    for k in range(NH):
        gather(F, k)

    for copy in weight_copies:
        copy.wait()
    for k in range(NH):
        arrived(X, k)
    complete(X)

    def tile(n):
        return pl.ds(pl.multiple_of(n * TILE, TILE), TILE)

    def project(a):
        def step(n, carry):
            gate[:, tile(n)] = dot(recv[a], wg[:, tile(n)])
            up[:, tile(n)] = dot(recv[a], wu[:, tile(n)])
            return carry

        lax.fori_loop(0, FF // TILE, step, 0)

    project(X)
    for k in range(NH):
        arrived(G, k)
        dispatch(F, k)
    complete(G)

    def backward(n, carry):
        grad = dot_nt(recv[G], wd[tile(n), :])
        value = gate[:, tile(n)]
        sigma = jax.nn.sigmoid(value)
        hid_a[:, tile(n)] = (grad * up[:, tile(n)] * sigma * (1.0 + value * (1.0 - sigma))).astype(BF)
        hid_b[:, tile(n)] = (grad * value * sigma).astype(BF)
        return carry

    lax.fori_loop(0, FF // TILE, backward, 0)

    def halves(a, k, product):
        first, width = TAIL[k]

        def step(n, carry):
            both = product(tile(n))
            own[a, :, tile(n)] = both[0:PLANE]
            sib_s[a, :, tile(n)] = both[PLANE:ROWS].astype(BF)
            return carry

        lax.fori_loop(first // TILE, (first + width) // TILE, step, 0)
        cols = pl.ds(first, width)
        remote(sib_s.at[a, :, cols], sib_r.at[a, :, cols], p_ss.at[a], p_rs.at[a, k], sibling).start()

    def give_back(a, k):
        cols = pl.ds(*TAIL[k])
        take(sib_r.at[a, :, cols], p_rs.at[a, k], sibling)
        total = (own[a, :, cols] + sib_r[a, :, cols].astype(F32)).astype(BF)
        ret_r[a, 0:SLOT, cols] = total[0:SLOT]
        ret_s[a, :, cols] = total[SLOT:PLANE]
        for i in range(1, NY):
            remote(
                ret_s.at[a, pl.ds((i - 1) * SLOT, SLOT), cols],
                ret_r.at[a, pl.ds(i * SLOT, SLOT), cols],
                r_ss.at[a], r_rs.at[a, k], downs[i],
            ).start()

    def results(a, product):
        for k in range(NT):
            halves(a, k, product)
            if k > 0:
                give_back(a, k - 1)
        give_back(a, NT - 1)

    results(B, lambda t: dot_nt(hid_a[...], wg[t, :]) + dot_nt(hid_b[...], wu[t, :]))

    for k in range(NH):
        arrived(F, k)
    complete(F)
    project(F)

    def activate(n, carry):
        value = gate[:, tile(n)]
        hid_a[:, tile(n)] = (value * jax.nn.sigmoid(value) * up[:, tile(n)]).astype(BF)
        return carry

    lax.fori_loop(0, FF // TILE, activate, 0)
    results(O, lambda t: dot(hid_a[...], wd[:, t]))

    def mixed(a, k):
        cols = pl.ds(*TAIL[k])
        take(ret_r.at[a, pl.ds(SLOT, PLANE - SLOT), cols], r_rs.at[a, k], downs[1])
        value = ret_r[a, :, cols]
        part[a, :, cols] = dot(mix_hi[a], value) + dot(mix_lo[a], value)

    def pass_on(a, k, block, add):
        cols = pl.ds(*TAIL[k])
        value = part[a, rows(block), cols]
        if add:
            take(rs_r.at[a, rows(block - 1), cols], c_rs.at[a, block - 1, k], behind)
            value = value + rs_r[a, rows(block - 1), cols].astype(F32)
        rs_s[a, rows(block - 1), cols] = value.astype(BF)
        if block <= 4:
            slot, device = (block - 2 if block > 1 else 3), behind
        else:
            slot, device = (block if block < 7 else 4), ahead
        remote(
            rs_s.at[a, rows(block - 1), cols], rs_r.at[a, rows(slot), cols],
            c_ss.at[a], c_rs.at[a, slot, k], device,
        ).start()

    def reduce_step(a, k, s):
        cols = pl.ds(*TAIL[k])
        if s == 0:
            mixed(a, k)
        if s < 4:
            pass_on(a, k, 4 - s, s > 0)
        if s < 3:
            pass_on(a, k, 5 + s, s > 0)
        if s == 4:
            take(rs_r.at[a, rows(3), cols], c_rs.at[a, 3, k], behind)
            take(rs_r.at[a, rows(4), cols], c_rs.at[a, 4, k], ahead)
            value = part[a, rows(0), cols]
            value = value + rs_r[a, rows(3), cols].astype(F32) + rs_r[a, rows(4), cols].astype(F32)
            xs[a, :, cols] = value.astype(BF)
            remote(
                xs.at[a, :, cols], xr.at[a, :, cols], x_ss.at[a], x_rs.at[a, k],
                x_next if a == O else x_prev,
            ).start()

    items = [(a, k) for a in (B, O) for k in range(NT)]
    for tick in range(len(items) + 4):
        for i, (a, k) in enumerate(items):
            s = tick - i
            if 0 <= s <= 4:
                reduce_step(a, k, s)

    sent(meta.at[pl.ds(0, 7 * TOK)], m_ss, behind)
    for a in (X, G, F):
        sent(ag.at[a, pl.ds(0, 7 * TOK)], z_ss.at[a], behind)
        sent(send.at[a], y_ss.at[a], behind)
        sent(recv.at[a, pl.ds(0, PLANE)], d_ss.at[a], behind)
    for a in (B, O):
        sent(sib_s.at[a], p_ss.at[a], behind)
        sent(ret_s.at[a], r_ss.at[a], behind)
        sent(rs_s.at[a], c_ss.at[a], behind)
    for a, out, empty in ((B, out_b, NX - 1), (O, out_f, 0)):
        for k in range(NT):
            take(xr.at[a, :, pl.ds(*TAIL[k])], x_rs.at[a, k], behind)
        out[...] = jnp.where(px == empty, jnp.zeros_like(out), xr[a])
        sent(xs.at[a], x_ss.at[a], behind)


def local(
    fwd_input, fwd_routes, fwd_weight, bwd_input, bwd_grad, bwd_routes, bwd_weight, w_gate, w_up, w_down
):
    vmem = pl.BlockSpec(memory_space=pltpu.VMEM)
    hbm = pl.BlockSpec(memory_space=pl.ANY)
    dma = pltpu.SemaphoreType.DMA
    out = jax.ShapeDtypeStruct((TOK, D), BF)
    fwd_next, grad_prev = pl.pallas_call(
        kernel,
        out_shape=(out, out),
        in_specs=[vmem] * 7 + [hbm] * 3,
        out_specs=(vmem, vmem),
        scratch_shapes=[
            pltpu.VMEM((D, FF), BF),
            pltpu.VMEM((D, FF), BF),
            pltpu.VMEM((FF, D), BF),
            pltpu.VMEM((GROUP, 128), F32),
            pltpu.VMEM((2, PLANE, GROUP), BF),
            pltpu.VMEM((2, GROUP, PLANE), BF),
            pltpu.VMEM((2, GROUP, PLANE), BF),
            pltpu.VMEM((3, GROUP, D), BF),
            pltpu.VMEM((3, PLANE - SLOT, D), BF),
            pltpu.VMEM((3, ROWS, D), BF),
            pltpu.VMEM((ROWS, FF), F32),
            pltpu.VMEM((ROWS, FF), F32),
            pltpu.VMEM((ROWS, FF), BF),
            pltpu.VMEM((ROWS, FF), BF),
            pltpu.VMEM((2, PLANE, D), F32),
            pltpu.VMEM((2, PLANE, D), BF),
            pltpu.VMEM((2, PLANE, D), BF),
            pltpu.VMEM((2, PLANE - SLOT, D), BF),
            pltpu.VMEM((2, PLANE, D), BF),
            pltpu.VMEM((2, GROUP, D), F32),
            pltpu.VMEM((2, 7 * TOK, D), BF),
            pltpu.VMEM((2, 7 * TOK, D), BF),
            pltpu.VMEM((2, TOK, D), BF),
            pltpu.VMEM((2, TOK, D), BF),
            dma((3,)),
            dma,
            dma((7,)),
            dma((3,)),
            dma((3, 7, NH)),
            dma((3,)),
            dma((3, NH)),
            dma((3,)),
            dma((3, NH)),
            dma((2,)),
            dma((2, NT)),
            dma((2,)),
            dma((2, NT)),
            dma((2,)),
            dma((2, 7, NT)),
            dma((2,)),
            dma((2, NT)),
        ],
        compiler_params=pltpu.CompilerParams(
            collective_id=0, has_side_effects=True, vmem_limit_bytes=60 * 2**20
        ),
        cost_estimate=pl.CostEstimate(
            flops=2 * 8 * ROWS * D * FF, bytes_accessed=3 * D * FF * 2, transcendentals=2 * ROWS * FF
        ),
    )(
        fwd_input[0], fwd_routes[0], fwd_weight[0], bwd_input[0], bwd_grad[0], bwd_routes[0], bwd_weight[0],
        w_gate[0, 0], w_up[0, 0], w_down[0, 0],
    )
    return fwd_next[None], grad_prev[None]


def solution(mesh):
    tokens = P("pipe", "expert", None)
    weights = P("pipe", "expert", None, None)
    return jax.shard_map(
        local,
        mesh=mesh,
        in_specs=(tokens,) * 7 + (weights,) * 3,
        out_specs=(tokens, tokens),
        check_vma=False,
    )
```

time: 641 us -> 139 us (0.22)
  waiting for transfers between devices: 519 us -> 0 us
  Pallas kernels: 0 us -> 127 us
  matrix products: 42 us -> 0 us
  starting transfers between devices: 41.5 us -> 0 us
  local copies, waits for them, and re-layouts: 26.1 us -> 8.51 us
  other arithmetic: 8.37 us -> 0 us
    all_to_all x5 -> x0, waiting for transfers between devices: 517 us -> none  [the longest x2 295 us: local(): lax.all_to_all(flat_groups(result), 'expert', split_axis=0, concat_axis=0...]
    pallas_call x0 -> x1, Pallas kernels: none -> 127 us  [local(): pl.pallas_call(kernel, out_shape=(out, out), in_specs=[vmem] * 7 + [hbm]...]
    dot_general x11 -> x0, matrix products: 42 us -> none  [the longest x1 9.82 us: expert_backward(): jnp.einsum('ngscf,gsdf->ngcd', gate_grad, gate_w, preferred_element_type=...]
    all_to_all x5 -> x0, starting transfers between devices: 36.8 us -> none  [the longest x2 13.1 us: local(): lax.all_to_all(flat_groups(result), 'expert', split_axis=0, concat_axis=0...]
    dot_general x1 -> x0, local copies, waits for them, and re-layouts: 8.8 us -> none  [expert_forward(): jnp.einsum('ngscf,gsfd->ngcd', hidden, down_w, preferred_element_type=jnp...]
    reduce_sum x6 -> x0, other arithmetic: 8.27 us -> none  [the longest x2 7.87 us: assemble_parts(): returned.reshape(E, copies, slot_count, width).sum(axis=1)]
    broadcast_in_dim x5 -> x0, local copies, waits for them, and re-layouts: 6.47 us -> none  [the longest x3 6.33 us: pack_rows(): jnp.broadcast_to(packed[:, None], (experts, SPLIT, capacity, feat_width))]
  transfers between devices with their start and end apart: 7 -> 0, of which waited for: 6 -> 0; matrix products, arithmetic and copies ran while one was open for 10% -> 0% of each run, Pallas kernels for 0% -> 0%
where the time goes in v1:
time: 139 us; the launch traced here: 136 us
  Pallas kernels  127 us (91%)
  local copies, waits for them, and re-layouts  8.51 us (6%)
    pallas_call x1, Pallas kernels, local(): pl.pallas_call(kernel, out_shape=(out, out), in_specs=[vmem] * 7 + [hbm]...  127 us
    unnamed x2, local copies, waits for them, and re-layouts  3.1 us

profile of v1, /device:TPU:8, one launch (start us, length us, event | category | flops | bytes accessed | tf_op | source)
XLA Modules:
  0.0 136.0 jit_solution(2241640583913934295)
XLA Ops:
  0.6 1.4 copy.12.rf
  2.0 1.4 copy.13.wf
  3.3 1.3 copy.14.rb
  4.7 1.3 copy.15.wb
  6.0 126.8 %shard_map.113 = (bf16[16,3584]{1,0:T(8,128)(2,1)}, bf16[16,3584]{1,0:T(8,128)(2,1)}) custom-call(bf16[16,3584]{1,0:T(8,128)(2,1)} %bitcast.21, s32[16,8]{1,0:T(8,128)} %copy.12.rf, f32[16,8]{1,0:T(8,128)} %copy.13.wf, bf16[16,3584]{1,0:T(8,128)(2,1)} %bitcast.22, bf16[16,3584]{1,0:T(8,128)(2,1)} %bitcast.23, s32[16,8]{1,0:T(8,128)} %copy.14.rb, ...), custom_call_target="tpu_custom_call" | custom-call | flops 11274289152 | bytes 11010048 | tf_op jit(solution)/shard_map/pallas_call | solution.py:386
  132.8 1.6 %copy.18 = bf16[1,16,3584]{2,1,0:T(8,128)(2,1)} copy(bf16[1,16,3584]{2,1,0:T(8,128)(2,1)} %bitcast.13) | data formatting | bytes 229376
  134.4 1.6 %copy.19 = bf16[1,16,3584]{2,1,0:T(8,128)(2,1)} copy(bf16[1,16,3584]{2,1,0:T(8,128)(2,1)} %bitcast.12) | data formatting | bytes 229376

commit v2 on v1

--- a/solution.py
+++ b/solution.py
@@ -43,25 +43,25 @@
 
 
 def slots_and_shares(routes, weights):
-    expert = lax.broadcasted_iota(jnp.int32, (TOK, 128), 1) & (E - 1)
-    hit = jnp.zeros((TOK, 128), F32)
-    share = jnp.zeros((TOK, 128), F32)
+    expert = lax.broadcasted_iota(jnp.int32, (128, TOK), 0) & (E - 1)
+    hit = jnp.zeros((128, TOK), F32)
+    share = jnp.zeros((128, TOK), F32)
     for k in range(TOP):
-        same = routes[:, k : k + 1] == expert
+        same = routes[k : k + 1, :] == expert
         hit = hit + jnp.where(same, 1.0, 0.0)
-        share = share + jnp.where(same, weights[:, k : k + 1], 0.0)
+        share = share + jnp.where(same, weights[k : k + 1, :], 0.0)
     rows = lax.broadcasted_iota(jnp.int32, (TOK, TOK), 0)
     cols = lax.broadcasted_iota(jnp.int32, (TOK, TOK), 1)
-    before = dot(jnp.where(rows > cols, 1.0, 0.0).astype(BF), hit.astype(BF))
+    before = dot(hit.astype(BF), jnp.where(rows < cols, 1.0, 0.0).astype(BF))
     return jnp.where(hit > 0.5, before, -1.0), share
 
 
 def kernel(
     xf, rf, wf, xb, gb, rb, wb, wg_h, wu_h, wd_h,
     out_f, out_b,
-    wg, wu, wd, meta, onehot, mix_hi, mix_lo, ag, send, recv,
+    wg, wu, wd, turned, meta, onehot, mix_hi, mix_lo, ag, send, recv,
     gate, up, hid_a, hid_b, own, sib_s, sib_r, ret_s, ret_r, part, rs_s, rs_r, xs, xr,
-    w_sem, m_ss, m_rs, z_ss, z_rs, y_ss, y_rs, d_ss, d_rs,
+    met, w_sem, m_ss, m_rs, z_ss, z_rs, y_ss, y_rs, d_ss, d_rs,
     p_ss, p_rs, r_ss, r_rs, c_ss, c_rs, x_ss, x_rs,
 ):
     px = lax.axis_index("pipe")
@@ -101,17 +101,31 @@
         copy.start()
 
     barrier = pltpu.get_barrier_semaphore()
-    partners = [ahead, behind, ups[1], ups[2], ups[3], sibling, x_next, x_prev]
+    partners = [ahead, behind, ups[1], ups[2], ups[3], x_next, x_prev]
     for device in partners:
         pl.semaphore_signal(barrier, inc=1, device_id=device, device_id_type=MESH)
 
-    lane = lax.broadcasted_iota(jnp.int32, (TOK, 128), 1)
+    @pl.when(c == 0)
+    def _():
+        pl.semaphore_signal(barrier, inc=1, device_id=sibling, device_id_type=MESH)
+
+    kind = lax.broadcasted_iota(jnp.int32, (128, TOK), 0)
     pos_f, share_f = slots_and_shares(rf[...], wf[...])
     pos_b, share_b = slots_and_shares(rb[...], wb[...])
-    meta[0:TOK, :] = jnp.where(
-        lane < E, pos_f, jnp.where(lane < 2 * E, share_f, jnp.where(lane < 3 * E, pos_b, share_b))
+    turned[:, 0:TOK] = jnp.where(
+        kind < E, pos_f, jnp.where(kind < 2 * E, share_f, jnp.where(kind < 3 * E, pos_b, share_b))
     )
-    pl.semaphore_wait(barrier, len(partners))
+    meta[0:TOK, :] = turned[...].T[0:TOK]
+    pl.semaphore_wait(barrier, len(partners) + c)
+
+    @pl.when(c == 1)
+    def _():
+        pl.semaphore_signal(met, inc=1, device_id=sibling, device_id_type=MESH)
+
+    def meet():
+        @pl.when(c == 0)
+        def _():
+            pl.semaphore_wait(met, 1)
 
     def rows(block):
         return pl.ds(block * TOK, TOK)
@@ -207,9 +221,8 @@
         for k in range(NH):
             take(recv.at[a, pl.ds(PLANE, PLANE), pl.ds(*HEAD[k])], d_rs.at[a, k], sibling)
 
-    for k in (0,):
-        meta_hop(0, 1, ahead)
-        meta_hop(0, 7, behind)
+    meta_hop(0, 1, ahead)
+    meta_hop(0, 7, behind)
     first_hops(X)
     ag[X, 0:TOK, :] = xb[...]
     ag[G, 0:TOK, :] = gb[...]
@@ -228,14 +241,15 @@
         dispatch(G, k)
     build(1)
     forward_hops(F)
-    for k in range(NH):
-        gather(F, k)
-
     for copy in weight_copies:
         copy.wait()
+    meet()
     for k in range(NH):
         arrived(X, k)
-    complete(X)
+    for k in range(NH):
+        gather(F, k)
+        dispatch(F, k)
+
 
     def tile(n):
         return pl.ds(pl.multiple_of(n * TILE, TILE), TILE)
@@ -248,10 +262,10 @@
 
         lax.fori_loop(0, FF // TILE, step, 0)
 
+    complete(X)
     project(X)
     for k in range(NH):
         arrived(G, k)
-        dispatch(F, k)
     complete(G)
 
     def backward(n, carry):
@@ -369,10 +383,10 @@
         sent(sib_s.at[a], p_ss.at[a], behind)
         sent(ret_s.at[a], r_ss.at[a], behind)
         sent(rs_s.at[a], c_ss.at[a], behind)
-    for a, out, empty in ((B, out_b, NX - 1), (O, out_f, 0)):
+    for a, out in ((B, out_b), (O, out_f)):
         for k in range(NT):
             take(xr.at[a, :, pl.ds(*TAIL[k])], x_rs.at[a, k], behind)
-        out[...] = jnp.where(px == empty, jnp.zeros_like(out), xr[a])
+        out[...] = xr[a]
         sent(xs.at[a], x_ss.at[a], behind)
 
 
@@ -392,6 +406,7 @@
             pltpu.VMEM((D, FF), BF),
             pltpu.VMEM((D, FF), BF),
             pltpu.VMEM((FF, D), BF),
+            pltpu.VMEM((128, 128), F32),
             pltpu.VMEM((GROUP, 128), F32),
             pltpu.VMEM((2, PLANE, GROUP), BF),
             pltpu.VMEM((2, GROUP, PLANE), BF),
@@ -413,6 +428,7 @@
             pltpu.VMEM((2, 7 * TOK, D), BF),
             pltpu.VMEM((2, TOK, D), BF),
             pltpu.VMEM((2, TOK, D), BF),
+            pltpu.SemaphoreType.REGULAR,
             dma((3,)),
             dma,
             dma((7,)),
@@ -438,9 +454,12 @@
             flops=2 * 8 * ROWS * D * FF, bytes_accessed=3 * D * FF * 2, transcendentals=2 * ROWS * FF
         ),
     )(
-        fwd_input[0], fwd_routes[0], fwd_weight[0], bwd_input[0], bwd_grad[0], bwd_routes[0], bwd_weight[0],
+        fwd_input[0], fwd_routes[0].T, fwd_weight[0].T, bwd_input[0], bwd_grad[0], bwd_routes[0].T, bwd_weight[0].T,
         w_gate[0, 0], w_up[0, 0], w_down[0, 0],
     )
+    px = lax.axis_index("pipe")
+    fwd_next = jnp.where(px == 0, jnp.zeros_like(fwd_next), fwd_next)
+    grad_prev = jnp.where(px == NX - 1, jnp.zeros_like(grad_prev), grad_prev)
     return fwd_next[None], grad_prev[None]
 
 

time: 139 us -> 126 us (0.906)
  local copies, waits for them, and re-layouts: 8.51 us -> 0 us
  Pallas kernels: 127 us -> 122 us
  other arithmetic: 0 us -> 1.62 us
    squeeze x4 -> x0, local copies, waits for them, and re-layouts: 5.4 us -> none  [the longest x1 1.36 us: local(): fwd_routes[0]]
    pallas_call x1, Pallas kernels: 127 us -> 122 us  [local(): pl.pallas_call(kernel, out_shape=(out, out), in_specs=[vmem] * 7 + [hbm]...]
    unnamed x2 -> x0, local copies, waits for them, and re-layouts: 3.1 us -> none
    broadcast_in_dim x0 -> x1, other arithmetic: none -> 1.62 us  [local(): return (fwd_next[None], grad_prev[None])]
where the time goes in v2:
time: 126 us; the launch traced here: 124 us
  Pallas kernels  122 us (97%)
  other arithmetic  1.62 us (1%)
    pallas_call x1, Pallas kernels, local(): pl.pallas_call(kernel, out_shape=(out, out), in_specs=[vmem] * 7 + [hbm]...  122 us

profile of v2, /device:TPU:8, one launch (start us, length us, event | category | flops | bytes accessed | tf_op | source)
XLA Modules:
  0.0 124.2 jit_solution(1635149784846505727)
XLA Ops:
  0.6 121.9 %shard_map.113 = (bf16[16,3584]{1,0:T(8,128)(2,1)}, bf16[16,3584]{1,0:T(8,128)(2,1)}) custom-call(bf16[16,3584]{1,0:T(8,128)(2,1)} %bitcast.25, s32[8,16]{1,0:T(8,128)} %bitcast.28, f32[8,16]{1,0:T(8,128)} %bitcast.29, bf16[16,3584]{1,0:T(8,128)(2,1)} %bitcast.26, bf16[16,3584]{1,0:T(8,128)(2,1)} %bitcast.27, s32[8,16]{1,0:T(8,128)} %bitcast.30, ...), custom_call_target="tpu_custom_call" | custom-call | flops 11274289152 | bytes 11010048 | tf_op jit(solution)/shard_map/pallas_call | solution.py:400
  122.6 1.6 %select_bitcast_fusion = (bf16[1,16,3584]{2,1,0:T(8,128)(2,1)}, bf16[1,16,3584]{2,1,0:T(8,128)(2,1)}) fusion(bf16[16,3584]{1,0:T(8,128)(2,1)} %get-tuple-element.5, pred[]{:T(512)S(6)} %eq.7, bf16[16,3584]{1,0:T(8,128)(2,1)} %get-tuple-element.4, pred[]{:T(512)S(6)} %eq.6), kind=kLoop, calls=%fused_computation | loop fusion | flops 114688 | bytes 458754 | tf_op jit(solution)/shard_map/broadcast_in_dim | solution.py:463

commit v3 on v2

--- a/solution.py
+++ b/solution.py
@@ -25,6 +25,7 @@
 ROWS = 2 * PLANE
 GROUP = NZ * TOK
 TILE = 256
+WIDE = 512
 
 HEAD = ((0, 512), (512, 1024), (1536, 1024), (2560, 1024))
 TAIL = ((0, 1024), (1024, 1024), (2048, 1024), (3072, 512))
@@ -61,7 +62,7 @@
     out_f, out_b,
     wg, wu, wd, turned, meta, onehot, mix_hi, mix_lo, ag, send, recv,
     gate, up, hid_a, hid_b, own, sib_s, sib_r, ret_s, ret_r, part, rs_s, rs_r, xs, xr,
-    met, w_sem, m_ss, m_rs, z_ss, z_rs, y_ss, y_rs, d_ss, d_rs,
+    met, o_sem, w_sem, m_ss, m_rs, z_ss, z_rs, y_ss, y_rs, d_ss, d_rs,
     p_ss, p_rs, r_ss, r_rs, c_ss, c_rs, x_ss, x_rs,
 ):
     px = lax.axis_index("pipe")
@@ -76,6 +77,8 @@
 
     ahead = at(px, z + turn, y, c)
     behind = at(px, z - turn, y, c)
+    ahead2 = at(px, z + 2 * turn, y, c)
+    behind2 = at(px, z - 2 * turn, y, c)
     ups = [None] + [at(px, z, y + i, c) for i in range(1, NY)]
     downs = [None] + [at(px, z, y - i, c) for i in range(1, NY)]
     sibling = at(px, z, y, 1 - c)
@@ -97,11 +100,14 @@
         pltpu.make_async_copy(a, b, w_sem.at[i])
         for i, (a, b) in enumerate(((wg_h, wg), (wu_h, wu), (wd_h, wd)))
     ]
-    for copy in weight_copies:
+    own_copies = [
+        pltpu.make_async_copy(src, ag.at[a, pl.ds(0, TOK)], o_sem.at[a]) for a, src in ((X, xb), (G, gb), (F, xf))
+    ]
+    for copy in own_copies + weight_copies:
         copy.start()
 
     barrier = pltpu.get_barrier_semaphore()
-    partners = [ahead, behind, ups[1], ups[2], ups[3], x_next, x_prev]
+    partners = [ahead, behind, ahead2, behind2, ups[1], ups[2], ups[3], x_next, x_prev]
     for device in partners:
         pl.semaphore_signal(barrier, inc=1, device_id=device, device_id_type=MESH)
 
@@ -133,6 +139,9 @@
     def meta_hop(src, dst, device):
         remote(meta.at[rows(src)], meta.at[rows(dst)], m_ss, m_rs.at[dst - 1], device).start()
 
+    def meta_landed(block):
+        take(meta.at[rows(block)], m_rs.at[block - 1], behind)
+
     def hop(a, src, dst, k, device):
         cols = pl.ds(*HEAD[k])
         block = (xb, gb, xf)[a].at[:, cols] if src == 0 else ag.at[a, rows(src), cols]
@@ -141,25 +150,18 @@
     def landed(a, block, k):
         take(ag.at[a, rows(block), pl.ds(*HEAD[k])], z_rs.at[a, block - 1, k], behind)
 
-    def first_hops(a):
-        for k in range(NH):
-            hop(a, 0, 1, k, ahead)
-            hop(a, 0, 7, k, behind)
-
-    def forward_hops(a, with_meta=False):
-        for s in (1, 2, 3):
-            if with_meta:
-                take(meta.at[rows(s)], m_rs.at[s - 1], behind)
-                meta_hop(s, s + 1, ahead)
-                take(meta.at[rows(8 - s)], m_rs.at[7 - s], ahead)
-                if s < 3:
-                    meta_hop(8 - s, 7 - s, behind)
-            for k in range(NH):
-                landed(a, s, k)
-                hop(a, s, s + 1, k, ahead)
-                landed(a, 8 - s, k)
-                if s < 3:
-                    hop(a, 8 - s, 7 - s, k, behind)
+    first = ((2, ahead2), (6, behind2), (1, ahead), (7, behind))
+    second = ((2, 4, ahead2), (2, 3, ahead), (6, 5, behind))
+
+    def first_hops(a, k):
+        for dst, device in first:
+            hop(a, 0, dst, k, device)
+
+    def second_hops(a, k):
+        landed(a, 2, k)
+        landed(a, 6, k)
+        for src, dst, device in second:
+            hop(a, src, dst, k, device)
 
     def build(which):
         every = meta[...]
@@ -195,7 +197,8 @@
     def gather(a, k):
         which = 1 if a == F else 0
         cols = pl.ds(*HEAD[k])
-        landed(a, 4, k)
+        for block in (1, 7, 3, 5, 4):
+            landed(a, block, k)
         picked = dot(onehot[which], ag[a, :, cols]).astype(BF)
         recv[a, 0:SLOT, cols] = picked[0:SLOT]
         send[a, :, cols] = picked[SLOT:PLANE]
@@ -221,38 +224,40 @@
         for k in range(NH):
             take(recv.at[a, pl.ds(PLANE, PLANE), pl.ds(*HEAD[k])], d_rs.at[a, k], sibling)
 
-    meta_hop(0, 1, ahead)
-    meta_hop(0, 7, behind)
-    first_hops(X)
-    ag[X, 0:TOK, :] = xb[...]
-    ag[G, 0:TOK, :] = gb[...]
-    ag[F, 0:TOK, :] = xf[...]
-    forward_hops(X, with_meta=True)
-    first_hops(G)
-    take(meta.at[rows(4)], m_rs.at[3], behind)
-    build(0)
-    for k in range(NH):
-        gather(X, k)
-        dispatch(X, k)
-    forward_hops(G)
-    first_hops(F)
-    for k in range(NH):
-        gather(G, k)
-        dispatch(G, k)
-    build(1)
-    forward_hops(F)
+    queue = [(a, k) for a in (X, G, F) for k in range(NH)]
+    for dst, device in first:
+        meta_hop(0, dst, device)
+    first_hops(*queue[0])
+    first_hops(*queue[1])
+    meta_landed(2)
+    meta_landed(6)
+    for src, dst, device in second:
+        meta_hop(src, dst, device)
+    for i, item in enumerate(queue):
+        second_hops(*item)
+        if i + 2 < len(queue):
+            first_hops(*queue[i + 2])
+        if i == 0:
+            for block in (1, 7, 3, 5, 4):
+                meta_landed(block)
+            build(0)
+            for copy in own_copies:
+                copy.wait()
+        if i > 0:
+            gather(*queue[i - 1])
+            dispatch(*queue[i - 1])
+        if i == NH:
+            build(1)
     for copy in weight_copies:
         copy.wait()
     meet()
     for k in range(NH):
         arrived(X, k)
-    for k in range(NH):
-        gather(F, k)
-        dispatch(F, k)
-
-
-    def tile(n):
-        return pl.ds(pl.multiple_of(n * TILE, TILE), TILE)
+    gather(*queue[-1])
+    dispatch(*queue[-1])
+
+    def tile(n, width=TILE):
+        return pl.ds(pl.multiple_of(n * width, width), width)
 
     def project(a):
         def step(n, carry):
@@ -282,12 +287,12 @@
         first, width = TAIL[k]
 
         def step(n, carry):
-            both = product(tile(n))
-            own[a, :, tile(n)] = both[0:PLANE]
-            sib_s[a, :, tile(n)] = both[PLANE:ROWS].astype(BF)
+            both = product(tile(n, WIDE))
+            own[a, :, tile(n, WIDE)] = both[0:PLANE]
+            sib_s[a, :, tile(n, WIDE)] = both[PLANE:ROWS].astype(BF)
             return carry
 
-        lax.fori_loop(first // TILE, (first + width) // TILE, step, 0)
+        lax.fori_loop(first // WIDE, (first + width) // WIDE, step, 0)
         cols = pl.ds(first, width)
         remote(sib_s.at[a, :, cols], sib_r.at[a, :, cols], p_ss.at[a], p_rs.at[a, k], sibling).start()
 
@@ -332,35 +337,35 @@
         value = ret_r[a, :, cols]
         part[a, :, cols] = dot(mix_hi[a], value) + dot(mix_lo[a], value)
 
-    def pass_on(a, k, block, add):
+    def pass_on(a, k, block, device, add=()):
         cols = pl.ds(*TAIL[k])
         value = part[a, rows(block), cols]
-        if add:
-            take(rs_r.at[a, rows(block - 1), cols], c_rs.at[a, block - 1, k], behind)
-            value = value + rs_r[a, rows(block - 1), cols].astype(F32)
+        for other in add:
+            take(rs_r.at[a, rows(other - 1), cols], c_rs.at[a, other - 1, k], behind)
+            value = value + rs_r[a, rows(other - 1), cols].astype(F32)
         rs_s[a, rows(block - 1), cols] = value.astype(BF)
-        if block <= 4:
-            slot, device = (block - 2 if block > 1 else 3), behind
-        else:
-            slot, device = (block if block < 7 else 4), ahead
         remote(
-            rs_s.at[a, rows(block - 1), cols], rs_r.at[a, rows(slot), cols],
-            c_ss.at[a], c_rs.at[a, slot, k], device,
+            rs_s.at[a, rows(block - 1), cols], rs_r.at[a, rows(block - 1), cols],
+            c_ss.at[a], c_rs.at[a, block - 1, k], device,
         ).start()
 
     def reduce_step(a, k, s):
         cols = pl.ds(*TAIL[k])
         if s == 0:
             mixed(a, k)
-        if s < 4:
-            pass_on(a, k, 4 - s, s > 0)
-        if s < 3:
-            pass_on(a, k, 5 + s, s > 0)
-        if s == 4:
-            take(rs_r.at[a, rows(3), cols], c_rs.at[a, 3, k], behind)
-            take(rs_r.at[a, rows(4), cols], c_rs.at[a, 4, k], ahead)
+            pass_on(a, k, 4, behind2)
+            pass_on(a, k, 5, ahead)
+            pass_on(a, k, 3, behind)
+            pass_on(a, k, 1, behind)
+            pass_on(a, k, 7, ahead)
+        if s == 1:
+            pass_on(a, k, 6, ahead2, (5,))
+            pass_on(a, k, 2, behind2, (3, 4))
+        if s == 2:
             value = part[a, rows(0), cols]
-            value = value + rs_r[a, rows(3), cols].astype(F32) + rs_r[a, rows(4), cols].astype(F32)
+            for block in (1, 7, 6, 2):
+                take(rs_r.at[a, rows(block - 1), cols], c_rs.at[a, block - 1, k], behind)
+                value = value + rs_r[a, rows(block - 1), cols].astype(F32)
             xs[a, :, cols] = value.astype(BF)
             remote(
                 xs.at[a, :, cols], xr.at[a, :, cols], x_ss.at[a], x_rs.at[a, k],
@@ -368,11 +373,10 @@
             ).start()
 
     items = [(a, k) for a in (B, O) for k in range(NT)]
-    for tick in range(len(items) + 4):
-        for i, (a, k) in enumerate(items):
-            s = tick - i
-            if 0 <= s <= 4:
-                reduce_step(a, k, s)
+    for tick in range(len(items) + 2):
+        for s in range(3):
+            if 0 <= tick - s < len(items):
+                reduce_step(*items[tick - s], s)
 
     sent(meta.at[pl.ds(0, 7 * TOK)], m_ss, behind)
     for a in (X, G, F):
@@ -400,7 +404,7 @@
     fwd_next, grad_prev = pl.pallas_call(
         kernel,
         out_shape=(out, out),
-        in_specs=[vmem] * 7 + [hbm] * 3,
+        in_specs=[hbm, vmem, vmem, hbm, hbm, vmem, vmem, hbm, hbm, hbm],
         out_specs=(vmem, vmem),
         scratch_shapes=[
             pltpu.VMEM((D, FF), BF),
@@ -429,6 +433,7 @@
             pltpu.VMEM((2, TOK, D), BF),
             pltpu.VMEM((2, TOK, D), BF),
             pltpu.SemaphoreType.REGULAR,
+            dma((3,)),
             dma((3,)),
             dma,
             dma((7,)),

time: 126 us -> 115 us (0.913); the launches traced: 124 us -> 115 us
  Pallas kernels: 122 us -> 113 us
    pallas_call x1, Pallas kernels: 122 us -> 113 us  [local(): pl.pallas_call(kernel, out_shape=(out, out), in_specs=[hbm, vmem, vmem, h...]
where the time goes in v3:
time: 115 us
  Pallas kernels  113 us (98%)
  other arithmetic  1.62 us (1%)
    pallas_call x1, Pallas kernels, local(): pl.pallas_call(kernel, out_shape=(out, out), in_specs=[hbm, vmem, vmem, h...  113 us

profile of v3, /device:TPU:8, one launch (start us, length us, event | category | flops | bytes accessed | tf_op | source)
XLA Modules:
  0.0 115.0 jit_solution(3901329502134922122)
XLA Ops:
  0.6 112.8 %shard_map.113 = (bf16[16,3584]{1,0:T(8,128)(2,1)}, bf16[16,3584]{1,0:T(8,128)(2,1)}) custom-call(bf16[16,3584]{1,0:T(8,128)(2,1)} %bitcast.25, s32[8,16]{1,0:T(8,128)} %bitcast.28, f32[8,16]{1,0:T(8,128)} %bitcast.29, bf16[16,3584]{1,0:T(8,128)(2,1)} %bitcast.26, bf16[16,3584]{1,0:T(8,128)(2,1)} %bitcast.27, s32[8,16]{1,0:T(8,128)} %bitcast.30, ...), custom_call_target="tpu_custom_call" | custom-call | flops 11274289152 | bytes 11010048 | tf_op jit(solution)/shard_map/pallas_call | solution.py:404
  113.4 1.6 %select_bitcast_fusion = (bf16[1,16,3584]{2,1,0:T(8,128)(2,1)}, bf16[1,16,3584]{2,1,0:T(8,128)(2,1)}) fusion(bf16[16,3584]{1,0:T(8,128)(2,1)} %get-tuple-element.5, pred[]{:T(512)S(6)} %eq.7, bf16[16,3584]{1,0:T(8,128)(2,1)} %get-tuple-element.4, pred[]{:T(512)S(6)} %eq.6), kind=kLoop, calls=%fused_computation | loop fusion | flops 114688 | bytes 458754 | tf_op jit(solution)/shard_map/broadcast_in_dim | solution.py:468

commit v4 on v3

--- a/solution.py
+++ b/solution.py
@@ -28,9 +28,10 @@
 WIDE = 512
 
 HEAD = ((0, 512), (512, 1024), (1536, 1024), (2560, 1024))
-TAIL = ((0, 1024), (1024, 1024), (2048, 1024), (3072, 512))
+TAIL = tuple((i * 512, 512) for i in range(7))
 NH = len(HEAD)
 NT = len(TAIL)
+LAG = 3
 X, G, F = 0, 1, 2
 B, O = 0, 1
 
@@ -61,9 +62,9 @@
     xf, rf, wf, xb, gb, rb, wb, wg_h, wu_h, wd_h,
     out_f, out_b,
     wg, wu, wd, turned, meta, onehot, mix_hi, mix_lo, ag, send, recv,
-    gate, up, hid_a, hid_b, own, sib_s, sib_r, ret_s, ret_r, part, rs_s, rs_r, xs, xr,
+    gate, up, hid_a, hid_b, own, sib_s, sib_r, ret_s, ret_r, part, rs_s, rs_r,
     met, o_sem, w_sem, m_ss, m_rs, z_ss, z_rs, y_ss, y_rs, d_ss, d_rs,
-    p_ss, p_rs, r_ss, r_rs, c_ss, c_rs, x_ss, x_rs,
+    p_ss, p_rs, r_ss, r_rs, c_ss, c_rs,
 ):
     px = lax.axis_index("pipe")
     e = lax.axis_index("expert")
@@ -82,8 +83,7 @@
     ups = [None] + [at(px, z, y + i, c) for i in range(1, NY)]
     downs = [None] + [at(px, z, y - i, c) for i in range(1, NY)]
     sibling = at(px, z, y, 1 - c)
-    x_next = at(px + 1, z, y, c)
-    x_prev = at(px - 1, z, y, c)
+    owners = [{i: at(px + step, z + i * turn, y, c) for i in (-2, -1, 0, 1, 2)} for step in (-1, 1)]
 
     def remote(src, dst, ss, rs, device):
         return pltpu.make_async_remote_copy(
@@ -107,7 +107,7 @@
         copy.start()
 
     barrier = pltpu.get_barrier_semaphore()
-    partners = [ahead, behind, ahead2, behind2, ups[1], ups[2], ups[3], x_next, x_prev]
+    partners = [ahead, behind, ahead2, behind2, ups[1], ups[2], ups[3], *owners[0].values(), *owners[1].values()]
     for device in partners:
         pl.semaphore_signal(barrier, inc=1, device_id=device, device_id_type=MESH)
 
@@ -243,11 +243,16 @@
             build(0)
             for copy in own_copies:
                 copy.wait()
-        if i > 0:
+        if i in (1, 2):
             gather(*queue[i - 1])
             dispatch(*queue[i - 1])
+        if i > 3:
+            gather(*queue[i - 2])
+            dispatch(*queue[i - 2])
         if i == NH:
             build(1)
+    gather(*queue[-2])
+    dispatch(*queue[-2])
     for copy in weight_copies:
         copy.wait()
     meet()
@@ -309,27 +314,11 @@
                 r_ss.at[a], r_rs.at[a, k], downs[i],
             ).start()
 
-    def results(a, product):
-        for k in range(NT):
-            halves(a, k, product)
-            if k > 0:
-                give_back(a, k - 1)
-        give_back(a, NT - 1)
-
-    results(B, lambda t: dot_nt(hid_a[...], wg[t, :]) + dot_nt(hid_b[...], wu[t, :]))
-
-    for k in range(NH):
-        arrived(F, k)
-    complete(F)
-    project(F)
-
-    def activate(n, carry):
-        value = gate[:, tile(n)]
-        hid_a[:, tile(n)] = (value * jax.nn.sigmoid(value) * up[:, tile(n)]).astype(BF)
-        return carry
-
-    lax.fori_loop(0, FF // TILE, activate, 0)
-    results(O, lambda t: dot(hid_a[...], wd[:, t]))
+    for k in range(NT):
+        halves(B, k, lambda t: dot_nt(hid_a[...], wg[t, :]) + dot_nt(hid_b[...], wu[t, :]))
+        if k > 0:
+            give_back(B, k - 1)
+    give_back(B, NT - 1)
 
     def mixed(a, k):
         cols = pl.ds(*TAIL[k])
@@ -341,12 +330,12 @@
         cols = pl.ds(*TAIL[k])
         value = part[a, rows(block), cols]
         for other in add:
-            take(rs_r.at[a, rows(other - 1), cols], c_rs.at[a, other - 1, k], behind)
-            value = value + rs_r[a, rows(other - 1), cols].astype(F32)
-        rs_s[a, rows(block - 1), cols] = value.astype(BF)
+            take(rs_r.at[a, rows(other), cols], c_rs.at[a, other, k], behind)
+            value = value + rs_r[a, rows(other), cols].astype(F32)
+        rs_s[a, rows(block), cols] = value.astype(BF)
         remote(
-            rs_s.at[a, rows(block - 1), cols], rs_r.at[a, rows(block - 1), cols],
-            c_ss.at[a], c_rs.at[a, block - 1, k], device,
+            rs_s.at[a, rows(block), cols], rs_r.at[a, rows(block), cols],
+            c_ss.at[a], c_rs.at[a, block, k], device,
         ).start()
 
     def reduce_step(a, k, s):
@@ -356,27 +345,47 @@
             pass_on(a, k, 4, behind2)
             pass_on(a, k, 5, ahead)
             pass_on(a, k, 3, behind)
-            pass_on(a, k, 1, behind)
-            pass_on(a, k, 7, ahead)
+            pass_on(a, k, 1, owners[a][-1])
+            pass_on(a, k, 7, owners[a][1])
+            pass_on(a, k, 0, owners[a][0])
         if s == 1:
-            pass_on(a, k, 6, ahead2, (5,))
-            pass_on(a, k, 2, behind2, (3, 4))
+            pass_on(a, k, 6, owners[a][2], (5,))
+            pass_on(a, k, 2, owners[a][-2], (3, 4))
         if s == 2:
-            value = part[a, rows(0), cols]
-            for block in (1, 7, 6, 2):
-                take(rs_r.at[a, rows(block - 1), cols], c_rs.at[a, block - 1, k], behind)
-                value = value + rs_r[a, rows(block - 1), cols].astype(F32)
-            xs[a, :, cols] = value.astype(BF)
-            remote(
-                xs.at[a, :, cols], xr.at[a, :, cols], x_ss.at[a], x_rs.at[a, k],
-                x_next if a == O else x_prev,
-            ).start()
+            value = jnp.zeros((TOK, TAIL[k][1]), F32)
+            for block in (0, 1, 7, 6, 2):
+                take(rs_r.at[a, rows(block), cols], c_rs.at[a, block, k], behind)
+                value = value + rs_r[a, rows(block), cols].astype(F32)
+            (out_b, out_f)[a][:, cols] = value.astype(BF)
 
     items = [(a, k) for a in (B, O) for k in range(NT)]
-    for tick in range(len(items) + 2):
+
+    def tick(t):
         for s in range(3):
-            if 0 <= tick - s < len(items):
-                reduce_step(*items[tick - s], s)
+            if 0 <= t - LAG * s < len(items):
+                reduce_step(*items[t - LAG * s], s)
+
+    for k in range(NH):
+        arrived(F, k)
+    complete(F)
+    project(F)
+    tick(0)
+
+    def activate(n, carry):
+        value = gate[:, tile(n)]
+        hid_a[:, tile(n)] = (value * jax.nn.sigmoid(value) * up[:, tile(n)]).astype(BF)
+        return carry
+
+    lax.fori_loop(0, FF // TILE, activate, 0)
+    for k in range(NT):
+        halves(O, k, lambda t: dot(hid_a[...], wd[:, t]))
+        if k > 0:
+            give_back(O, k - 1)
+            if k < NT - 1:
+                tick(k)
+    give_back(O, NT - 1)
+    for t in range(NT - 1, len(items) + 2 * LAG):
+        tick(t)
 
     sent(meta.at[pl.ds(0, 7 * TOK)], m_ss, behind)
     for a in (X, G, F):
@@ -387,11 +396,6 @@
         sent(sib_s.at[a], p_ss.at[a], behind)
         sent(ret_s.at[a], r_ss.at[a], behind)
         sent(rs_s.at[a], c_ss.at[a], behind)
-    for a, out in ((B, out_b), (O, out_f)):
-        for k in range(NT):
-            take(xr.at[a, :, pl.ds(*TAIL[k])], x_rs.at[a, k], behind)
-        out[...] = xr[a]
-        sent(xs.at[a], x_ss.at[a], behind)
 
 
 def local(
@@ -428,10 +432,8 @@
             pltpu.VMEM((2, PLANE - SLOT, D), BF),
             pltpu.VMEM((2, PLANE, D), BF),
             pltpu.VMEM((2, GROUP, D), F32),
-            pltpu.VMEM((2, 7 * TOK, D), BF),
-            pltpu.VMEM((2, 7 * TOK, D), BF),
-            pltpu.VMEM((2, TOK, D), BF),
-            pltpu.VMEM((2, TOK, D), BF),
+            pltpu.VMEM((2, GROUP, D), BF),
+            pltpu.VMEM((2, GROUP, D), BF),
             pltpu.SemaphoreType.REGULAR,
             dma((3,)),
             dma((3,)),
@@ -448,9 +450,7 @@
             dma((2,)),
             dma((2, NT)),
             dma((2,)),
-            dma((2, 7, NT)),
-            dma((2,)),
-            dma((2, NT)),
+            dma((2, 8, NT)),
         ],
         compiler_params=pltpu.CompilerParams(
             collective_id=0, has_side_effects=True, vmem_limit_bytes=60 * 2**20

time: 115 us -> 111 us (0.965)
  Pallas kernels: 113 us -> 108 us
    pallas_call x1, Pallas kernels: 113 us -> 108 us  [local(): pl.pallas_call(kernel, out_shape=(out, out), in_specs=[hbm, vmem, vmem, h...]
where the time goes in v4:
time: 111 us
  Pallas kernels  108 us (97%)
  other arithmetic  1.62 us (1%)
    pallas_call x1, Pallas kernels, local(): pl.pallas_call(kernel, out_shape=(out, out), in_specs=[hbm, vmem, vmem, h...  108 us

profile of v4, /device:TPU:8, one launch (start us, length us, event | category | flops | bytes accessed | tf_op | source)
XLA Modules:
  0.0 110.5 jit_solution(10279989221994650329)
XLA Ops:
  0.6 108.3 %shard_map.113 = (bf16[16,3584]{1,0:T(8,128)(2,1)}, bf16[16,3584]{1,0:T(8,128)(2,1)}) custom-call(bf16[16,3584]{1,0:T(8,128)(2,1)} %bitcast.25, s32[8,16]{1,0:T(8,128)} %bitcast.28, f32[8,16]{1,0:T(8,128)} %bitcast.29, bf16[16,3584]{1,0:T(8,128)(2,1)} %bitcast.26, bf16[16,3584]{1,0:T(8,128)(2,1)} %bitcast.27, s32[8,16]{1,0:T(8,128)} %bitcast.30, ...), custom_call_target="tpu_custom_call" | custom-call | flops 11274289152 | bytes 11010048 | tf_op jit(solution)/shard_map/pallas_call | solution.py:408
  108.9 1.6 %select_bitcast_fusion = (bf16[1,16,3584]{2,1,0:T(8,128)(2,1)}, bf16[1,16,3584]{2,1,0:T(8,128)(2,1)}) fusion(bf16[16,3584]{1,0:T(8,128)(2,1)} %get-tuple-element.5, pred[]{:T(512)S(6)} %eq.7, bf16[16,3584]{1,0:T(8,128)(2,1)} %get-tuple-element.4, pred[]{:T(512)S(6)} %eq.6), kind=kLoop, calls=%fused_computation | loop fusion | flops 114688 | bytes 458754 | tf_op jit(solution)/shard_map/broadcast_in_dim | solution.py:468

commit v5 on v4

--- a/solution.py
+++ b/solution.py
@@ -384,8 +384,12 @@
             if k < NT - 1:
                 tick(k)
     give_back(O, NT - 1)
-    for t in range(NT - 1, len(items) + 2 * LAG):
+    for t in range(NT - 1, len(items)):
         tick(t)
+    for i in range(len(items) - LAG, len(items)):
+        reduce_step(*items[i], 1)
+    for i in range(len(items) - 2 * LAG, len(items)):
+        reduce_step(*items[i], 2)
 
     sent(meta.at[pl.ds(0, 7 * TOK)], m_ss, behind)
     for a in (X, G, F):

time: 111 us -> 110 us (level)
  no operation moved by 1% of the time
where the time goes in v5:
time: 110 us
  Pallas kernels  108 us (98%)
  other arithmetic  1.62 us (1%)
    pallas_call x1, Pallas kernels, local(): pl.pallas_call(kernel, out_shape=(out, out), in_specs=[hbm, vmem, vmem, h...  108 us

profile of v5, /device:TPU:8, one launch (start us, length us, event | category | flops | bytes accessed | tf_op | source)
XLA Modules:
  0.0 110.0 jit_solution(12616586819248420996)
XLA Ops:
  0.6 107.7 %shard_map.113 = (bf16[16,3584]{1,0:T(8,128)(2,1)}, bf16[16,3584]{1,0:T(8,128)(2,1)}) custom-call(bf16[16,3584]{1,0:T(8,128)(2,1)} %bitcast.25, s32[8,16]{1,0:T(8,128)} %bitcast.28, f32[8,16]{1,0:T(8,128)} %bitcast.29, bf16[16,3584]{1,0:T(8,128)(2,1)} %bitcast.26, bf16[16,3584]{1,0:T(8,128)(2,1)} %bitcast.27, s32[8,16]{1,0:T(8,128)} %bitcast.30, ...), custom_call_target="tpu_custom_call" | custom-call | flops 11274289152 | bytes 11010048 | tf_op jit(solution)/shard_map/pallas_call | solution.py:412
  108.4 1.6 %select_bitcast_fusion = (bf16[1,16,3584]{2,1,0:T(8,128)(2,1)}, bf16[1,16,3584]{2,1,0:T(8,128)(2,1)}) fusion(bf16[16,3584]{1,0:T(8,128)(2,1)} %get-tuple-element.5, pred[]{:T(512)S(6)} %eq.7, bf16[16,3584]{1,0:T(8,128)(2,1)} %get-tuple-element.4, pred[]{:T(512)S(6)} %eq.6), kind=kLoop, calls=%fused_computation | loop fusion | flops 114688 | bytes 458754 | tf_op jit(solution)/shard_map/broadcast_in_dim | solution.py:472
